TPU v7x, 256 devices: a whole 4x4x8 slice. The times are simulated.
256 devices in a mesh: ctx: 64 (over y, z, x_lo), ch: 4 (over x_hi, core).
Axes of the slice: x: 4 (x_hi: 2, x_lo: 2; x = x_hi * 2 + x_lo), y: 4, z: 8, core: 2. Of those that a mesh axis runs over, the one named last changes fastest.
Arguments:
- base_ids: int32 [8192], P('ctx'), may hold values from 0 to 511
- base_table: bfloat16 [512, 3, 4096], P(None, None, 'ch'), may hold values from -6 to 6
- short_taps: float32 [3, 3, 4096], P(None, None, 'ch'), may hold values from -2.4 to 2.4
- mode_rates: float32 [16, 4096], P(None, 'ch'), may hold values from 3e-05 to 0.1
- mode_residues: float32 [16, 4096], P(None, 'ch'), may hold values from -1.8 to 1.8
- skip_gain: float32 [4096], P('ch'), may hold values from 0.5 to 1.5
- out_weight: bfloat16 [4096, 8192], P('ctx', 'ch'), may hold values from -0.09375 to 0.09375
Outputs:
- mixed: bfloat16 [8192, 8192], P('ctx', 'ch')
All inputs are finite; a program needn't handle non-finite values.
Results may differ from a plain program's by a relative error of at most 0.013.
Values may be sent and summed in bfloat16 or wider, within the bound.
A program may use at most 128 MiB of HBM per device.

v0:
```python
import jax
import jax.numpy as jnp
from jax import lax
from jax.sharding import PartitionSpec as P

block_len = 32


def shifted(value, axis, steps):
    count = lax.axis_size(axis)
    leading, last = (max(0, -steps), min(count, count - steps))
    return lax.ppermute(value, axis, [(source, source + steps) for source in range(leading, last)])


def chain(earlier, later):
    return (earlier[0] * later[0], earlier[1] * later[0] + later[1])


def mode_tables(rates, residues):
    coef = residues * jnp.sqrt(2.0 * rates)
    lags = jnp.arange(block_len).astype(jnp.float32)
    decay = jnp.exp(-rates[:, :, None] * lags[None, None, :])
    filt = jnp.sum(coef[:, :, None] * decay, axis=0)
    offset = jnp.arange(block_len)[:, None] - jnp.arange(block_len)[None, :]
    toeplitz = jnp.where(offset[None, :, :] >= 0, filt[:, jnp.clip(offset, 0, block_len - 1)], 0.0)
    end_weight = jnp.exp(-rates[:, :, None] * (block_len - 1 - lags)[None, None, :])
    out_weight_modes = coef[:, :, None] * jnp.exp(-rates[:, :, None] * (lags + 1.0)[None, None, :])
    return (toeplitz, end_weight, out_weight_modes)


def block_pass(signal, rates, tables):
    toeplitz, end_weight, out_modes = tables
    width, length = signal.shape
    blocks = length // block_len
    shaped = signal.reshape(width, blocks, block_len)
    inner = jnp.einsum("cts,cbs->cbt", toeplitz, shaped, precision=lax.Precision.HIGHEST)
    ends = jnp.einsum("rcs,cbs->rcb", end_weight, shaped, precision=lax.Precision.HIGHEST)
    steps = jnp.broadcast_to(jnp.exp(-rates * block_len)[:, :, None], ends.shape)
    scanned = lax.associative_scan(chain, (steps, ends), axis=2)[1]
    before = jnp.concatenate([jnp.zeros_like(scanned[:, :, :1]), scanned[:, :, :-1]], axis=2)
    index_f = jnp.arange(blocks).astype(jnp.float32)
    decay_before = jnp.exp(-rates[:, :, None] * (block_len * index_f)[None, None, :])
    return (inner, before, decay_before, scanned[:, :, -1])


def finish(parts, start, out_modes):
    inner, before, decay_before, last = parts
    width, blocks = (inner.shape[0], inner.shape[1])
    states = before + decay_before * start[:, :, None]
    outer = jnp.einsum("rct,rcb->cbt", out_modes, states, precision=lax.Precision.HIGHEST)
    return (inner + outer).reshape(width, blocks * block_len)


def body(base_ids, base_table, short_taps, mode_rates, mode_residues, skip_gain, out_weight):
    rows = jnp.take(base_table, base_ids, axis=0)
    prior = shifted(rows[-2:], "ctx", 1)
    padded = jnp.concatenate([prior, rows], axis=0).astype(jnp.float32)
    feat = short_taps[0] * padded[2:] + short_taps[1] * padded[1:-1] + short_taps[2] * padded[:-2]
    query = feat[:, 0]
    product = (feat[:, 1] * feat[:, 2]).astype(jnp.bfloat16)
    product_f = product.astype(jnp.float32)
    local_ch = product.shape[1]
    sub_width = local_ch // lax.axis_size("ctx")
    first = lax.axis_index("ctx") * sub_width
    rates_sub = lax.dynamic_slice_in_dim(mode_rates, first, sub_width, 1)
    residues_sub = lax.dynamic_slice_in_dim(mode_residues, first, sub_width, 1)
    whole = lax.all_to_all(product.T, "ctx", split_axis=0, concat_axis=1, tiled=True).astype(
        jnp.float32
    )
    tables = mode_tables(rates_sub, residues_sub)
    parts = block_pass(whole, rates_sub, tables)
    convolved_ch = finish(parts, jnp.zeros_like(rates_sub), tables[2])
    convolved = lax.all_to_all(convolved_ch, "ctx", split_axis=1, concat_axis=0, tiled=True).T
    gated = (query * (convolved + skip_gain * product_f)).astype(jnp.bfloat16)
    gathered = lax.all_gather(gated, "ch", axis=1, tiled=True)
    total = jnp.dot(
        gathered,
        lax.all_gather(out_weight, "ctx", axis=0, tiled=True),
        preferred_element_type=jnp.float32,
    )
    return total.astype(jnp.bfloat16)


def solution(mesh):
    in_specs = (
        P("ctx"),
        P(None, None, "ch"),
        P(None, None, "ch"),
        P(None, "ch"),
        P(None, "ch"),
        P("ch"),
        P("ctx", "ch"),
    )
    out_specs = P("ctx", "ch")
    return jax.shard_map(body, mesh=mesh, in_specs=in_specs, out_specs=out_specs, check_vma=False)
```

profile of v0, /device:TPU:8, one launch (start us, length us, event | category | flops | bytes accessed | tf_op | source)
XLA Modules:
  0.0 696.0 jit_solution(5693877176848301776)
XLA Ops:
  8.4 3.9 gather_fusion
  14.5 3.4 collective-permute-start
  28.6 12.5 %all-to-all-start = ((bf16[64,16,128]{2,1,0:T(8,128)(2,1)}), bf16[64,16,128]{2,1,0:T(8,128)(2,1)S(1)}, u32[]{:S(2)}, u32[]{:S(2)}) async-start(bf16[64,16,128]{2,1,0:T(8,128)(2,1)} %bitcast.55), calls=%async_computation | async-start | bytes 524288 | tf_op jit(solution)/shard_map/all_to_all | solution.py:67
  41.6 4.0 gather_fusion.1
  45.7 2.0 copy.91
  49.4 3.0 all-to-all-done
  55.5 2.2 convolution_bitcast_fusion
  57.7 4.5 slice.211
  62.2 5.1 slice.213
  68.3 2.3 slice.215
  70.7 3.0 slice.217
  74.6 1.8 slice.219
  76.5 1.9 slice.221
  82.0 1.7 multiply_add_fusion.3
  83.7 1.8 slice.227
  85.6 1.9 slice.229
  87.5 1.7 multiply_add_fusion.2
  89.2 1.7 slice.231
  90.9 1.7 slice.233
  97.1 1.8 slice.249
  99.0 2.1 slice.252
  101.1 1.8 slice.255
  102.9 2.9 slice.258
  105.8 5.9 slice.261
  115.4 6.2 pad.53
  121.6 1.7 pad_maximum_fusion
  123.4 8.8 %pad.52 = f32[16,16,4]{2,0,1:T(8,128)} pad(f32[16,16,2]{2,0,1:T(8,128)} %pad_maximum_fusion, f32[]{:T(128)} %constant.9.clone.1), padding=0_0_0x0_0_0x0_1_1 | pad | bytes 6148 | tf_op jit(solution)/shard_map/pad | solution.py:39
  135.8 6.1 pad.54
  141.9 8.8 %pad.55 = f32[16,16,8]{2,0,1:T(8,128)} pad(f32[16,16,4]{2,0,1:T(8,128)} %add.170, f32[]{:T(128)} %constant.9.clone.1), padding=0_0_0x0_0_0x1_0_1 | pad | bytes 12292 | tf_op jit(solution)/shard_map/pad | solution.py:39
  152.3 8.9 %pad.57 = f32[16,16,16]{2,0,1:T(8,128)} pad(f32[16,16,8]{2,0,1:T(8,128)} %add.172, f32[]{:T(128)} %constant.9.clone.1), padding=0_0_0x0_0_0x1_0_1 | pad | bytes 24580 | tf_op jit(solution)/shard_map/pad | solution.py:39
  164.0 8.9 %pad.56 = f32[16,16,16]{2,0,1:T(8,128)} pad(f32[16,16,8]{2,0,1:T(8,128)} %pad_maximum_fusion.2, f32[]{:T(128)} %constant.9.clone.1), padding=0_0_0x0_0_0x0_1_1 | pad | bytes 24580 | tf_op jit(solution)/shard_map/pad | solution.py:39
  176.4 6.5 pad.58
  182.9 9.0 %pad.59 = f32[16,16,32]{2,0,1:T(8,128)} pad(f32[16,16,16]{2,0,1:T(8,128)} %add.174, f32[]{:T(128)} %constant.9.clone.1), padding=0_0_0x0_0_0x1_0_1 | pad | bytes 49156 | tf_op jit(solution)/shard_map/pad | solution.py:39
  193.4 9.2 %pad.61 = f32[16,16,64]{2,0,1:T(8,128)} pad(f32[16,16,32]{2,0,1:T(8,128)} %add.176, f32[]{:T(128)} %constant.9.clone.1), padding=0_0_0x0_0_0x1_0_1 | pad | bytes 98308 | tf_op jit(solution)/shard_map/pad | solution.py:39
  203.8 2.1 pad.60
  208.7 3.2 pad.62
  211.9 7.4 %pad.63 = f32[16,16,128]{2,0,1:T(8,128)S(1)} pad(f32[16,16,64]{2,0,1:T(8,128)} %add.178, f32[]{:T(128)} %constant.9.clone.1), padding=0_0_0x0_0_0x1_0_1 | pad | bytes 196612 | tf_op jit(solution)/shard_map/pad | solution.py:39
  220.0 10.5 %pad.108 = f32[16,16,256]{2,0,1:T(8,128)} pad(f32[16,16,128]{2,0,1:T(8,128)} %add.180, f32[]{:T(128)} %constant.9.clone.1), padding=0_0_0x0_0_0x1_0_1 | pad | bytes 393220
  232.3 10.5 %pad.85 = f32[16,16,255]{2,0,1:T(8,128)} pad(f32[16,16,128]{2,0,1:T(8,128)} %pad_maximum_fusion.6, f32[]{:T(128)} %constant.9.clone.1), padding=0_0_0x0_0_0x0_0_1 | pad | bytes 392196 | tf_op jit(solution)/shard_map/slice | solution.py:40
  245.5 1.9 convolution_add_fusion
  247.5 3.0 copy.110
  250.5 2.7 all_to_all.29
  254.5 24.2 %all_to_all.35 = f32[16,64,128]{2,0,1:T(8,128)} all-to-all(f32[16,64,128]{2,0,1:T(8,128)S(1)} %copy.111), channel_id=1, replica_groups=mesh['ctx'=64,'ch'=4] {'ctx'}, dimensions={1} | all-to-all | bytes 1048576 | tf_op jit(solution)/shard_map/all_to_all | solution.py:73
  278.7 2.0 copy.112
  280.8 2.4 fusion.4
  283.9 19.8 %all-gather.3.cloned.1.call-done = bf16[128,4096]{1,0:T(8,128)(2,1)} async-done(((bf16[128,1024]{1,0:T(8,128)(2,1)}), bf16[128,4096]{1,0:T(8,128)(2,1)}) %all-gather.3.cloned.1.call-update) | async-done | bytes 1048592 | tf_op jit(solution)/shard_map/all_gather | solution.py:75
  303.7 376.2 %all-gather.5.cloned.1.call-done = bf16[4096,2048]{1,0:T(8,128)(2,1)} async-done(((bf16[64,2048]{1,0:T(8,128)(2,1)}), bf16[4096,2048]{1,0:T(8,128)(2,1)}) %all-gather.5.cloned.1.call-update) | async-done | bytes 16777232 | tf_op jit(solution)/shard_map/all_gather | solution.py:78
  679.9 9.2 %convolution_convert_fusion = bf16[128,2048]{1,0:T(8,128)(2,1)} fusion(bf16[128,4096]{1,0:T(8,128)(2,1)} %all-gather.3.cloned.1.call-done, bf16[4096,2048]{1,0:T(8,128)(2,1)} %all-gather.5.cloned.1.call-done), kind=kOutput, calls=%fused_computation.2 | convolution fusion | flops 2147745792 | bytes 18350080 | tf_op jit(solution)/shard_map/dot_general | solution.py:76
  (106 shorter events, 58.3 us)
Async XLA Ops:
  6.5 1.9 copy-start
  12.3 5.6 copy-start.12
  13.6 0.9 copy-start.5
  14.5 10.2 %collective-permute-start = (bf16[2,3,1024]{2,0,1:T(2,128)(2,1)S(1)}, bf16[2,3,1024]{2,0,1:T(2,128)(2,1)S(1)}, u32[]{:S(2)}, u32[]{:S(2)}) collective-permute-start(bf16[2,3,1024]{2,0,1:T(2,128)(2,1)S(1)} %slice.267), channel_id=1, source_target_pairs={{0,4},{4,8},{8,12},{12,16},{16,20},{20,24},{24,28},{28,32},{32,36}... | collective-permute-start | bytes 36872 | tf_op jit(solution)/shard_map/ppermute | solution.py:12
  24.7 16.7 %copy-start.10 = (f32[16,16]{0,1:T(8,128)}, f32[16,16]{0,1:T(8,128)S(1)}, u32[]{:S(2)}) copy-start(f32[16,16]{0,1:T(8,128)S(1)} %copy.88) | copy-start | bytes 3076
  26.6 1.1 copy-start.1
  28.6 23.7 %all-to-all-start = ((bf16[64,16,128]{2,1,0:T(8,128)(2,1)}), bf16[64,16,128]{2,1,0:T(8,128)(2,1)S(1)}, u32[]{:S(2)}, u32[]{:S(2)}) async-start(bf16[64,16,128]{2,1,0:T(8,128)(2,1)} %bitcast.55), calls=%async_computation | async-start | bytes 524288 | tf_op jit(solution)/shard_map/all_to_all | solution.py:67
  41.2 262.6 %all-gather.3.cloned.1.call-start = ((), (), s32[]{:S(2)}) async-start(), calls=%async_computation.2 | async-start | bytes 1310720 | tf_op jit(solution)/shard_map/all_gather | solution.py:75
  52.4 0.7 copy-start.8
  57.7 4.5 copy-start.6
  79.4 11.5 %copy-start.3 = (f32[16,16,32]{2,0,1:T(8,128)}, f32[16,16,32]{2,0,1:T(8,128)S(1)}, u32[]{:S(2)}) copy-start(f32[16,16,32]{2,0,1:T(8,128)S(1)} %multiply_add_fusion.4) | copy-start | bytes 98308
  111.7 2.9 copy-start.9
  141.9 33.8 %copy-start.4 = (f32[16,16,32]{2,0,1:T(8,128)S(1)}, f32[16,16,32]{2,0,1:T(8,128)}, u32[]{:S(2)}) copy-start(f32[16,16,32]{2,0,1:T(8,128)} %copy-done.3) | copy-start | bytes 98308
  205.9 25.6 %slice-start = ((f32[16,16,256]{2,0,1:T(8,128)}), f32[16,16,1]{2,0,1:T(8,128)S(1)}, s32[]{:S(2)}) async-start(f32[16,16,256]{2,0,1:T(8,128)} %copy-done.6), calls=%async_computation.4 | async-start | bytes 262144 | tf_op jit(solution)/shard_map/slice | solution.py:39
  231.5 12.5 %copy-start.11 = (f32[16,16]{0,1:T(8,128)S(1)}, f32[16,16]{0,1:T(8,128)}, u32[]{:S(2)}) copy-start(f32[16,16]{0,1:T(8,128)} %copy-done.10) | copy-start | bytes 3076
  231.5 14.0 %copy-start.7 = (f32[32,32,16]{1,0,2:T(8,128)S(1)}, f32[32,32,16]{1,0,2:T(8,128)}, u32[]{:S(2)}) copy-start(f32[32,32,16]{1,0,2:T(8,128)} %copy.91) | copy-start | bytes 196612
  232.3 13.2 %copy-start.13 = (pred[32,32]{1,0:T(8,128)(4,1)S(1)}, pred[32,32]{1,0:T(8,128)(4,1)}, u32[]{:S(2)}) copy-start(pred[32,32]{1,0:T(8,128)(4,1)} %subtract_compare_fusion) | copy-start | bytes 3076
  242.8 2.8 copy-start.2
  253.1 27.6 %copy-start.14 = (f32[1024]{0:T(1024)S(1)}, f32[1024]{0:T(1024)}, u32[]{:S(2)}) copy-start(f32[1024]{0:T(1024)} %param.12) | copy-start | bytes 12292
  283.2 396.8 %all-gather.5.cloned.1.call-start = ((), (), s32[]{:S(2)}) async-start(), calls=%async_computation.3 | async-start | bytes 17039360 | tf_op jit(solution)/shard_map/all_gather | solution.py:78
Sparse Core Ops, SparseCore 0:
  283.3 20.3 all-gather.2
  305.5 374.3 all-gather.4
where the time goes:
time: 703 us; the launch traced here: 696 us
  waiting for transfers between devices  400 us (57%)
  local copies, waits for them, and re-layouts  184 us (26%)
  other arithmetic  43.5 us (6%)
  blocking collectives  24.2 us (3%)
  starting transfers between devices  16.2 us (2%)
  matrix products  14.9 us (2%)
  between operations  13.8 us (2%)
    all_gather x1, waiting for transfers between devices, body(): lax.all_gather(out_weight, 'ctx', axis=0, tiled=True)  376 us
    pad x12, local copies, waits for them, and re-layouts, block_pass(): scanned = lax.associative_scan(chain, (steps, ends), axis=2)[1]  85 us
    slice x24, local copies, waits for them, and re-layouts, block_pass(): scanned = lax.associative_scan(chain, (steps, ends), axis=2)[1]  48 us
    all_to_all x1, blocking collectives, body(): lax.all_to_all(convolved_ch, 'ctx', split_axis=1, concat_axis=0, tiled=True)  24.2 us
    all_gather x1, waiting for transfers between devices, body(): gathered = lax.all_gather(gated, 'ch', axis=1, tiled=True)  19.8 us
    add x14, other arithmetic, chain(): return (earlier[0] * later[0], earlier[1] * later[0] + later[1])  16.1 us
  transfers between devices with their start and end apart: 4, of which 3 were waited for; matrix products, arithmetic and copies ran while one was open for 2% of the time, Pallas kernels for 0%

commit v1 on v0

--- a/solution.py
+++ b/solution.py
@@ -72,7 +72,9 @@
     convolved_ch = finish(parts, jnp.zeros_like(rates_sub), tables[2])
     convolved = lax.all_to_all(convolved_ch, "ctx", split_axis=1, concat_axis=0, tiled=True).T
     gated = (query * (convolved + skip_gain * product_f)).astype(jnp.bfloat16)
-    gathered = lax.all_gather(gated, "ch", axis=1, tiled=True)
+    gathered = jnp.concatenate(
+        lax.all_to_all(jnp.stack([gated] * lax.axis_size("ch")), "ch", 0, 0), axis=1
+    )
     total = jnp.dot(
         gathered,
         lax.all_gather(out_weight, "ctx", axis=0, tiled=True),

time: 703 us -> 429 us (0.61)
  the two profiles are of different devices: /device:TPU:8 before, /device:TPU:1 now
where the time goes in v1:
time: 429 us; the launch traced here: 421 us
  local copies, waits for them, and re-layouts  192 us (45%)
  blocking collectives  73.2 us (17%)
  waiting for transfers between devices  69.4 us (16%)
  other arithmetic  41.3 us (10%)
  starting transfers between devices  16.4 us (4%)
  matrix products  14.9 us (3%)
  between operations  13.8 us (3%)
    pad x12, local copies, waits for them, and re-layouts, block_pass(): scanned = lax.associative_scan(chain, (steps, ends), axis=2)[1]  90.3 us
    all_gather x1, waiting for transfers between devices, body(): lax.all_gather(out_weight, 'ctx', axis=0, tiled=True)  65.2 us
    slice x24, local copies, waits for them, and re-layouts, block_pass(): scanned = lax.associative_scan(chain, (steps, ends), axis=2)[1]  48 us
    all_to_all x1, blocking collectives, body(): lax.all_to_all(jnp.stack([gated] * lax.axis_size('ch')), 'ch', 0, 0)  46.5 us
    all_to_all x1, blocking collectives, body(): lax.all_to_all(convolved_ch, 'ctx', split_axis=1, concat_axis=0, tiled=True)  26.7 us
    add x14, other arithmetic, chain(): return (earlier[0] * later[0], earlier[1] * later[0] + later[1])  16.2 us
    unnamed x37, local copies, waits for them, and re-layouts  14.2 us
    all_to_all x1, starting transfers between devices, body(): lax.all_to_all(product.T, 'ctx', split_axis=0, concat_axis=1, tiled=True)  12.4 us
  transfers between devices with their start and end apart: 3, of which 2 were waited for; matrix products, arithmetic and copies ran while one was open for 55% of the time, Pallas kernels for 0%

profile of v1, /device:TPU:1, one launch (start us, length us, event | category | flops | bytes accessed | tf_op | source)
XLA Modules:
  0.0 420.7 jit_solution(5321413987224938235)
XLA Ops:
  8.4 3.9 gather_fusion
  14.5 3.9 collective-permute-start
  29.2 12.4 %all-to-all-start = ((bf16[64,16,128]{2,1,0:T(8,128)(2,1)}), bf16[64,16,128]{2,1,0:T(8,128)(2,1)S(1)}, u32[]{:S(2)}, u32[]{:S(2)}) async-start(bf16[64,16,128]{2,1,0:T(8,128)(2,1)} %bitcast.59), calls=%async_computation | async-start | bytes 524288 | tf_op jit(solution)/shard_map/all_to_all | solution.py:67
  41.9 4.0 gather_fusion.1
  45.9 2.0 copy.94
  49.6 3.5 all-to-all-done
  56.2 2.2 convolution_bitcast_fusion
  58.4 4.5 %slice.211 = f32[16,16,128]{2,0,1:T(8,128)S(1)} slice(f32[16,16,256]{2,0,1:T(8,128)S(1)} %convolution_bitcast_fusion), slice={[0:16:1], [0:16:1], [0:255:2]} | slice | bytes 262144 | tf_op jit(solution)/shard_map/slice | solution.py:39
  62.9 5.1 %slice.213 = f32[16,16,128]{2,0,1:T(8,128)} slice(f32[16,16,256]{2,0,1:T(8,128)S(1)} %convolution_bitcast_fusion), slice={[0:16:1], [0:16:1], [1:256:2]} | slice | bytes 262144 | tf_op jit(solution)/shard_map/slice | solution.py:39
  69.0 2.3 slice.215
  71.3 3.0 slice.217
  75.3 1.8 slice.219
  77.1 1.9 slice.221
  82.7 1.7 multiply_add_fusion.3
  84.4 1.8 slice.227
  86.3 1.9 slice.229
  88.2 1.7 multiply_add_fusion.2
  89.9 1.7 slice.231
  91.6 1.7 slice.233
  96.1 1.7 slice.246
  97.8 1.8 slice.249
  99.6 2.1 slice.252
  101.8 1.8 slice.255
  103.6 2.9 slice.258
  106.5 5.9 %slice.261 = f32[16,16,127]{2,0,1:T(8,128)} slice(f32[16,16,256]{2,0,1:T(8,128)} %copy-done.7), slice={[0:16:1], [0:16:1], [2:256:2]} | slice | bytes 260096 | tf_op jit(solution)/shard_map/slice | solution.py:39
  116.0 8.8 %pad.53 = f32[16,16,4]{2,0,1:T(8,128)} pad(f32[16,16,2]{2,0,1:T(8,128)} %pad_add_fusion, f32[]{:T(128)} %constant.9.clone.1), padding=0_0_0x0_0_0x1_0_1 | pad | bytes 6148 | tf_op jit(solution)/shard_map/pad | solution.py:39
  126.7 8.8 %pad.52 = f32[16,16,4]{2,0,1:T(8,128)} pad(f32[16,16,2]{2,0,1:T(8,128)} %pad_maximum_fusion, f32[]{:T(128)} %constant.9.clone.1), padding=0_0_0x0_0_0x0_1_1 | pad | bytes 6148 | tf_op jit(solution)/shard_map/pad | solution.py:39
  139.0 8.8 %pad.54 = f32[16,16,8]{2,0,1:T(8,128)} pad(f32[16,16,4]{2,0,1:T(8,128)} %pad_maximum_fusion.1, f32[]{:T(128)} %constant.9.clone.1), padding=0_0_0x0_0_0x0_1_1 | pad | bytes 12292 | tf_op jit(solution)/shard_map/pad | solution.py:39
  147.8 8.8 %pad.55 = f32[16,16,8]{2,0,1:T(8,128)} pad(f32[16,16,4]{2,0,1:T(8,128)} %add.170, f32[]{:T(128)} %constant.9.clone.1), padding=0_0_0x0_0_0x1_0_1 | pad | bytes 12292 | tf_op jit(solution)/shard_map/pad | solution.py:39
  158.3 8.9 %pad.57 = f32[16,16,16]{2,0,1:T(8,128)} pad(f32[16,16,8]{2,0,1:T(8,128)} %add.172, f32[]{:T(128)} %constant.9.clone.1), padding=0_0_0x0_0_0x1_0_1 | pad | bytes 24580 | tf_op jit(solution)/shard_map/pad | solution.py:39
  170.0 8.9 %pad.56 = f32[16,16,16]{2,0,1:T(8,128)} pad(f32[16,16,8]{2,0,1:T(8,128)} %pad_maximum_fusion.2, f32[]{:T(128)} %constant.9.clone.1), padding=0_0_0x0_0_0x0_1_1 | pad | bytes 24580 | tf_op jit(solution)/shard_map/pad | solution.py:39
  182.4 6.5 %pad.58 = f32[16,16,32]{2,0,1:T(8,128)S(1)} pad(f32[16,16,16]{2,0,1:T(8,128)} %pad_maximum_fusion.3, f32[]{:T(128)} %constant.9.clone.1), padding=0_0_0x0_0_0x0_1_1 | pad | bytes 49156 | tf_op jit(solution)/shard_map/pad | solution.py:39
  188.9 9.0 %pad.59 = f32[16,16,32]{2,0,1:T(8,128)} pad(f32[16,16,16]{2,0,1:T(8,128)} %add.174, f32[]{:T(128)} %constant.9.clone.1), padding=0_0_0x0_0_0x1_0_1 | pad | bytes 49156 | tf_op jit(solution)/shard_map/pad | solution.py:39
  199.4 9.2 %pad.61 = f32[16,16,64]{2,0,1:T(8,128)} pad(f32[16,16,32]{2,0,1:T(8,128)} %add.176, f32[]{:T(128)} %constant.9.clone.1), padding=0_0_0x0_0_0x1_0_1 | pad | bytes 98308 | tf_op jit(solution)/shard_map/pad | solution.py:39
  209.8 2.1 pad.60
  214.7 3.2 pad.62
  217.9 7.4 %pad.63 = f32[16,16,128]{2,0,1:T(8,128)S(1)} pad(f32[16,16,64]{2,0,1:T(8,128)} %add.178, f32[]{:T(128)} %constant.9.clone.1), padding=0_0_0x0_0_0x1_0_1 | pad | bytes 196612 | tf_op jit(solution)/shard_map/pad | solution.py:39
  226.0 10.5 %pad.108 = f32[16,16,256]{2,0,1:T(8,128)} pad(f32[16,16,128]{2,0,1:T(8,128)} %add.180, f32[]{:T(128)} %constant.9.clone.1), padding=0_0_0x0_0_0x1_0_1 | pad | bytes 393220
  238.2 10.5 %pad.85 = f32[16,16,255]{2,0,1:T(8,128)} pad(f32[16,16,128]{2,0,1:T(8,128)} %pad_maximum_fusion.6, f32[]{:T(128)} %constant.9.clone.1), padding=0_0_0x0_0_0x0_0_1 | pad | bytes 392196 | tf_op jit(solution)/shard_map/slice | solution.py:40
  251.5 1.9 convolution_add_fusion
  253.4 3.0 copy.113
  256.4 2.7 all_to_all.32
  260.4 26.7 %all_to_all.40 = f32[16,64,128]{2,0,1:T(8,128)} all-to-all(f32[16,64,128]{2,0,1:T(8,128)S(1)} %copy.114), channel_id=1, replica_groups=mesh['ctx'=64,'ch'=4] {'ctx'}, dimensions={1} | all-to-all | bytes 1048576 | tf_op jit(solution)/shard_map/all_to_all | solution.py:73
  287.2 2.0 copy.115
  289.2 1.7 fusion.4
  292.8 46.5 %all_to_all.41 = bf16[4,128,1024]{1,2,0:T(8,128)(2,1)} all-to-all(bf16[4,128,1024]{1,2,0:T(8,128)(2,1)S(1)} %stack.2), channel_id=1, replica_groups=mesh['ctx'=64,'ch'=4] {'ch'}, dimensions={0} | all-to-all | bytes 2097152 | tf_op jit(solution)/shard_map/all_to_all | solution.py:76
  339.3 65.2 %all-gather.2.cloned.1.call-done = bf16[4096,2048]{1,0:T(8,128)(2,1)} async-done(((bf16[64,2048]{1,0:T(8,128)(2,1)}), bf16[4096,2048]{1,0:T(8,128)(2,1)}) %all-gather.2.cloned.1.call-update) | async-done | bytes 16777232 | tf_op jit(solution)/shard_map/all_gather | solution.py:80
  404.6 9.3 %convolution_convert_fusion = bf16[128,2048]{1,0:T(8,128)(2,1)} fusion(bf16[128,4096]{0,1:T(8,128)(2,1)} %bitcast.50, bf16[4096,2048]{1,0:T(8,128)(2,1)} %all-gather.2.cloned.1.call-done), kind=kOutput, calls=%fused_computation.2 | convolution fusion | flops 2147745792 | bytes 18350080 | tf_op jit(solution)/shard_map/dot_general | solution.py:78
  (112 shorter events, 59.0 us)
Async XLA Ops:
  6.5 1.9 copy-start
  6.5 398.0 %all-gather.2.cloned.1.call-start = ((), (), s32[]{:S(2)}) async-start(), calls=%async_computation.3 | async-start | bytes 17039360 | tf_op jit(solution)/shard_map/all_gather | solution.py:80
  8.4 3.9 copy-start.17
  12.3 7.1 %copy-start.14 = (f32[3,3,1024]{2,1,0:T(4,128)S(1)}, f32[3,3,1024]{2,1,0:T(4,128)}, u32[]{:S(2)}) copy-start(f32[3,3,1024]{2,1,0:T(4,128)} %param.9) | copy-start | bytes 110596
  13.6 0.9 copy-start.6
  14.5 10.8 %collective-permute-start = (bf16[2,3,1024]{2,0,1:T(2,128)(2,1)S(1)}, bf16[2,3,1024]{2,0,1:T(2,128)(2,1)S(1)}, u32[]{:S(2)}, u32[]{:S(2)}) collective-permute-start(bf16[2,3,1024]{2,0,1:T(2,128)(2,1)S(1)} %slice.267), channel_id=1, source_target_pairs={{0,4},{4,8},{8,12},{12,16},{16,20},{20,24},{24,28},{28,32},{32,36}... | collective-permute-start | bytes 36872 | tf_op jit(solution)/shard_map/ppermute | solution.py:12
  25.3 16.4 %copy-start.12 = (f32[16,16]{0,1:T(8,128)}, f32[16,16]{0,1:T(8,128)S(1)}, u32[]{:S(2)}) copy-start(f32[16,16]{0,1:T(8,128)S(1)} %copy.91) | copy-start | bytes 3076
  27.1 1.1 copy-start.1
  29.2 23.9 %all-to-all-start = ((bf16[64,16,128]{2,1,0:T(8,128)(2,1)}), bf16[64,16,128]{2,1,0:T(8,128)(2,1)S(1)}, u32[]{:S(2)}, u32[]{:S(2)}) async-start(bf16[64,16,128]{2,1,0:T(8,128)(2,1)} %bitcast.59), calls=%async_computation | async-start | bytes 524288 | tf_op jit(solution)/shard_map/all_to_all | solution.py:67
  53.0 0.7 copy-start.11
  58.4 4.5 %copy-start.7 = (f32[16,16,256]{2,0,1:T(8,128)}, f32[16,16,256]{2,0,1:T(8,128)S(1)}, u32[]{:S(2)}) copy-start(f32[16,16,256]{2,0,1:T(8,128)S(1)} %convolution_bitcast_fusion) | copy-start | bytes 786436
  80.1 11.6 %copy-start.3 = (f32[16,16,32]{2,0,1:T(8,128)}, f32[16,16,32]{2,0,1:T(8,128)S(1)}, u32[]{:S(2)}) copy-start(f32[16,16,32]{2,0,1:T(8,128)S(1)} %multiply_add_fusion.4) | copy-start | bytes 98308
  114.5 0.6 copy-start.8
  114.5 0.7 copy-start.9
  125.9 12.3 %copy-start.5 = (f32[16,16,8]{2,0,1:T(8,128)S(1)}, f32[16,16,8]{2,0,1:T(8,128)}, u32[]{:S(2)}) copy-start(f32[16,16,8]{2,0,1:T(8,128)} %multiply_add_fusion.2) | copy-start | bytes 24580
  147.8 33.8 %copy-start.4 = (f32[16,16,32]{2,0,1:T(8,128)S(1)}, f32[16,16,32]{2,0,1:T(8,128)}, u32[]{:S(2)}) copy-start(f32[16,16,32]{2,0,1:T(8,128)} %copy-done.3) | copy-start | bytes 98308
  211.9 25.5 %slice-start = ((f32[16,16,256]{2,0,1:T(8,128)}), f32[16,16,1]{2,0,1:T(8,128)S(1)}, s32[]{:S(2)}) async-start(f32[16,16,256]{2,0,1:T(8,128)} %copy-done.7), calls=%async_computation.4 | async-start | bytes 262144 | tf_op jit(solution)/shard_map/slice | solution.py:39
  237.5 12.4 %copy-start.13 = (f32[16,16]{0,1:T(8,128)S(1)}, f32[16,16]{0,1:T(8,128)}, u32[]{:S(2)}) copy-start(f32[16,16]{0,1:T(8,128)} %copy-done.12) | copy-start | bytes 3076
  237.5 14.0 %copy-start.10 = (f32[32,32,16]{1,0,2:T(8,128)S(1)}, f32[32,32,16]{1,0,2:T(8,128)}, u32[]{:S(2)}) copy-start(f32[32,32,16]{1,0,2:T(8,128)} %copy.94) | copy-start | bytes 196612
  238.2 13.2 %copy-start.15 = (pred[32,32]{1,0:T(8,128)(4,1)S(1)}, pred[32,32]{1,0:T(8,128)(4,1)}, u32[]{:S(2)}) copy-start(pred[32,32]{1,0:T(8,128)(4,1)} %subtract_compare_fusion) | copy-start | bytes 3076
  248.7 2.7 copy-start.2
  259.1 30.1 %copy-start.16 = (f32[1024]{0:T(1024)S(1)}, f32[1024]{0:T(1024)}, u32[]{:S(2)}) copy-start(f32[1024]{0:T(1024)} %param.12) | copy-start | bytes 12292
Sparse Core Ops, SparseCore 0:
  9.1 395.3 all-gather.1
